TPU v7x, 32 devices: a whole 2x2x4 slice. The times are simulated.
32 devices in a mesh: row: 8 (over y, x, core), col: 4 (over z).
Axes of the slice: x: 2, y: 2, z: 4, core: 2. Of those that a mesh axis runs over, the one named last changes fastest.
Arguments:
- sensitivity: float32 [16384, 16384], P('row', 'col'), as said below
- injection: float32 [16384, 1024], P('col', 'row'), may hold values from -6 to 6
- dispatch_now: float32 [16384, 1024], P('row', 'col'), may hold values from -3 to 3
- limit_class: int32 [16384], P('row'), may hold values from 0 to 15
- box_table: float32 [16], replicated, may hold values from 0.3 to 1.5
- owner_index: int32 [16384, 1], P('row'), may hold values from 0 to 7; in each aligned block of 2048 rows (0 to 2047, 2048 to 4095, ...) at most 768 rows name the same one
- member_slot: int32 [16384], P('row'), may hold values from 0 to 127
- agg_limit: float32 [1024], P('row'), may hold values from 0.5 to 4
Outputs:
- dispatch: float32 [16384, 1024], P('row', 'col')
- aggregate: float32 [1024, 1024], P('row', 'col')
Inputs may be any that keep to these rules, and one draw needn't show every extreme that they name: `sensitivity`: symmetric. `owner_index`: in each aligned block of 2048 inverters (those of one index of row) at most 768 have the same owner, and some owner has exactly 768 in some block.
All inputs are finite; a program needn't handle non-finite values.
Results may differ from a plain program's by a relative error of at most 0.000088.
Values sent between devices are 32-bit elements; how exact they have to be, the bound alone decides.
A program may use at most 128 MiB of HBM per device.

v0:
```python
import jax
import jax.numpy as jnp
from jax import lax
from jax.sharding import PartitionSpec as P

step_size = 0.1
chunks = 4


def rounded(x):
    return lax.reduce_precision(x, exponent_bits=8, mantissa_bits=7)


def split3(x):
    hi = rounded(x)
    rest = x - hi
    mid = rounded(rest)
    return tuple((part.astype(jnp.bfloat16) for part in (hi, mid, rest - mid)))


def body(
    sensitivity,
    injection,
    dispatch_now,
    limit_class,
    box_table,
    owner_index,
    member_slot,
    agg_limit,
):
    owners = lax.axis_size("row")
    agg_dev = agg_limit.shape[0]
    row_count = sensitivity.shape[0]
    injection_t = injection.T
    width = injection_t.shape[0] // chunks
    group = owners // lax.axis_size("col")
    gradients = []
    for chunk in range(chunks):
        part = injection_t[chunk * width : (chunk + 1) * width]
        part = lax.all_gather(part, "row", axis=0, tiled=True)
        partial_value = lax.dot_general(
            part,
            sensitivity,
            (((1,), (1,)), ((), ())),
            precision=lax.Precision.HIGH,
            preferred_element_type=jnp.float32,
        )
        summed = lax.psum_scatter(partial_value, "col", scatter_dimension=0, tiled=True)
        gradients.append(summed.reshape(group, width, row_count))
    gradient = 2.0 * jnp.concatenate(gradients, axis=1).reshape(-1, row_count).T
    classes = jnp.arange(box_table.shape[0], dtype=jnp.int32)
    box_bound = jnp.sum(
        jnp.where(limit_class[:, None] == classes[None, :], box_table[None, :], 0.0), axis=1
    )[:, None]
    stepped = jnp.clip(dispatch_now - step_size * gradient, -box_bound, box_bound)
    agg_id = owner_index[:, 0] * agg_dev + member_slot
    aggs = owners * agg_dev
    selector = (agg_id[None, :] == jnp.arange(aggs, dtype=jnp.int32)[:, None]).astype(jnp.bfloat16)

    def pick(left, parts, dims):
        return sum(
            (
                lax.dot_general(left, part, (dims, ((), ())), preferred_element_type=jnp.float32)
                for part in parts
            )
        )

    local = pick(selector, split3(stepped), ((1,), (0,)))
    total = lax.psum_scatter(local, "row", scatter_dimension=0, tiled=True)
    limit_col = agg_limit[:, None]
    factor = limit_col / jnp.maximum(jnp.abs(total), limit_col)
    aggregate = total * factor
    all_factor = lax.all_gather(factor, "row", axis=0, tiled=True)
    own_factor = pick(selector, split3(all_factor), ((0,), (0,)))
    return (stepped * own_factor, aggregate)


def solution(mesh):
    placed = (
        P("row", "col"),
        P("col", "row"),
        P("row", "col"),
        P("row"),
        P(),
        P("row", None),
        P("row"),
        P("row"),
    )
    return jax.shard_map(
        body,
        mesh=mesh,
        in_specs=placed,
        out_specs=(P("row", "col"), P("row", "col")),
        check_vma=False,
    )
```

profile of v0, /device:TPU:0, one launch (start us, length us, event | category | flops | bytes accessed | tf_op | source)
XLA Modules:
  0.0 439.6 jit_solution(8798306970045158717)
XLA Ops:
  7.2 1.9 copy.13
  12.6 37.5 %all-gather.6.cloned.1.call-done = f32[256,4096]{1,0:T(8,128)} async-done(((f32[32,4096]{1,0:T(8,128)}), f32[256,4096]{1,0:T(8,128)}) %all-gather.6.cloned.1.call-update) | async-done | bytes 4194320 | tf_op jit(solution)/shard_map/all_gather | solution.py:40
  50.1 20.0 %fusion.25 = f32[256,2048]{1,0:T(8,128)} fusion(f32[256,4096]{1,0:T(8,128)} %all-gather.6.cloned.1.call-done, f32[2048,4096]{1,0:T(8,128)} %param.8), kind=kOutput, calls=%fused_computation.38 | convolution fusion | flops 12884901888 | bytes 39845888 | tf_op jit(solution)/shard_map/dot_general | solution.py:41
  70.2 18.6 %all-gather.8.cloned.1.call-done = f32[256,4096]{1,0:T(8,128)} async-done(((f32[32,4096]{1,0:T(8,128)}), f32[256,4096]{1,0:T(8,128)}) %all-gather.8.cloned.1.call-update) | async-done | bytes 4194320 | tf_op jit(solution)/shard_map/all_gather | solution.py:40
  88.8 20.0 %fusion.26 = f32[256,2048]{1,0:T(8,128)} fusion(f32[256,4096]{1,0:T(8,128)} %all-gather.8.cloned.1.call-done, f32[2048,4096]{1,0:T(8,128)} %param.8), kind=kOutput, calls=%fused_computation.39 | convolution fusion | flops 12884901888 | bytes 39845888 | tf_op jit(solution)/shard_map/dot_general | solution.py:41
  109.1 18.4 %all-gather.10.cloned.1.call-done = f32[256,4096]{1,0:T(8,128)} async-done(((f32[32,4096]{1,0:T(8,128)}), f32[256,4096]{1,0:T(8,128)}) %all-gather.10.cloned.1.call-update) | async-done | bytes 4194320 | tf_op jit(solution)/shard_map/all_gather | solution.py:40
  127.5 20.0 %fusion.27 = f32[256,2048]{1,0:T(8,128)} fusion(f32[256,4096]{1,0:T(8,128)} %all-gather.10.cloned.1.call-done, f32[2048,4096]{1,0:T(8,128)} %param.8), kind=kOutput, calls=%fused_computation.40 | convolution fusion | flops 12884901888 | bytes 39845888 | tf_op jit(solution)/shard_map/dot_general | solution.py:41
  147.5 18.4 %all-gather.12.cloned.1.call-done = f32[256,4096]{1,0:T(8,128)} async-done(((f32[32,4096]{1,0:T(8,128)}), f32[256,4096]{1,0:T(8,128)}) %all-gather.12.cloned.1.call-update) | async-done | bytes 4194320 | tf_op jit(solution)/shard_map/all_gather | solution.py:40
  166.0 19.8 %fusion.28 = f32[256,2048]{1,0:T(8,128)} fusion(f32[256,4096]{1,0:T(8,128)} %all-gather.12.cloned.1.call-done, f32[2048,4096]{1,0:T(8,128)} %param.8), kind=kOutput, calls=%fused_computation.41 | convolution fusion | flops 12884901888 | bytes 39845888 | tf_op jit(solution)/shard_map/dot_general | solution.py:41
  186.7 25.3 %reduce-scatter.6.cloned.1.call-done = f32[64,2048]{1,0:T(8,128)} async-done(((f32[256,2048]{1,0:T(8,128)}), f32[64,2048]{1,0:T(8,128)}) %reduce-scatter.6.cloned.1.call-update) | async-done | bytes 524304 | tf_op jit(solution)/shard_map/reduce_scatter | solution.py:48
  212.0 45.5 %reduce-scatter.8.cloned.1.call-done = f32[64,2048]{1,0:T(8,128)} async-done(((f32[256,2048]{1,0:T(8,128)}), f32[64,2048]{1,0:T(8,128)}) %reduce-scatter.8.cloned.1.call-update) | async-done | bytes 524304 | tf_op jit(solution)/shard_map/reduce_scatter | solution.py:48
  257.5 45.5 %reduce-scatter.10.cloned.1.call-done = f32[64,2048]{1,0:T(8,128)} async-done(((f32[256,2048]{1,0:T(8,128)}), f32[64,2048]{1,0:T(8,128)}) %reduce-scatter.10.cloned.1.call-update) | async-done | bytes 524304 | tf_op jit(solution)/shard_map/reduce_scatter | solution.py:48
  303.0 46.2 %reduce-scatter.12.cloned.1.call-done = f32[64,2048]{1,0:T(8,128)} async-done(((f32[256,2048]{1,0:T(8,128)}), f32[64,2048]{1,0:T(8,128)}) %reduce-scatter.12.cloned.1.call-update) | async-done | bytes 524304 | tf_op jit(solution)/shard_map/reduce_scatter | solution.py:48
  349.2 3.1 maximum_multiply_fusion
  352.3 1.9 copy.15
  354.2 1.9 fusion.17
  356.2 1.7 fusion.3
  359.5 2.5 fusion.19
  362.4 35.2 %reduce-scatter.14.cloned.1.call-done = f32[128,256]{1,0:T(8,128)} async-done(((f32[1024,256]{1,0:T(8,128)}), f32[128,256]{1,0:T(8,128)}) %reduce-scatter.14.cloned.1.call-update) | async-done | bytes 131088 | tf_op jit(solution)/shard_map/reduce_scatter | solution.py:69
  397.6 1.7 fusion.23
  399.3 23.6 %all-gather.14.cloned.1.call-done = f32[1024,256]{1,0:T(8,128)} async-done(((f32[128,256]{1,0:T(8,128)}), f32[1024,256]{1,0:T(8,128)}) %all-gather.14.cloned.1.call-update) | async-done | bytes 1048592 | tf_op jit(solution)/shard_map/all_gather | solution.py:73
  422.9 3.7 fusion.1
  426.6 2.4 fusion.12
  429.1 3.7 fusion.14
  (42 shorter events, 6.5 us)
Async XLA Ops:
  7.2 42.9 %all-gather.6.cloned.1.call-start = ((), (), s32[]{:S(2)}) async-start(), calls=%async_computation.5 | async-start | bytes 4718592 | tf_op jit(solution)/shard_map/all_gather | solution.py:40
  10.5 78.3 %all-gather.8.cloned.1.call-start = ((), (), s32[]{:S(2)}) async-start(), calls=%async_computation.7 | async-start | bytes 4718592 | tf_op jit(solution)/shard_map/all_gather | solution.py:40
  11.3 116.2 %all-gather.10.cloned.1.call-start = ((), (), s32[]{:S(2)}) async-start(), calls=%async_computation.9 | async-start | bytes 4718592 | tf_op jit(solution)/shard_map/all_gather | solution.py:40
  12.0 154.0 %all-gather.12.cloned.1.call-start = ((), (), s32[]{:S(2)}) async-start(), calls=%async_computation.11 | async-start | bytes 4718592 | tf_op jit(solution)/shard_map/all_gather | solution.py:40
  12.6 199.4 %reduce-scatter.6.cloned.1.call-start = ((), (), s32[]{:S(2)}) async-start(), calls=%async_computation.6 | async-start | bytes 2621440 | tf_op jit(solution)/shard_map/reduce_scatter | solution.py:48
  70.2 187.3 %reduce-scatter.8.cloned.1.call-start = ((), (), s32[]{:S(2)}) async-start(), calls=%async_computation.8 | async-start | bytes 2621440 | tf_op jit(solution)/shard_map/reduce_scatter | solution.py:48
  108.9 194.1 %reduce-scatter.10.cloned.1.call-start = ((), (), s32[]{:S(2)}) async-start(), calls=%async_computation.10 | async-start | bytes 2621440 | tf_op jit(solution)/shard_map/reduce_scatter | solution.py:48
  147.5 201.7 %reduce-scatter.12.cloned.1.call-start = ((), (), s32[]{:S(2)}) async-start(), calls=%async_computation.12 | async-start | bytes 2621440 | tf_op jit(solution)/shard_map/reduce_scatter | solution.py:48
  185.8 0.7 copy-start.3
  185.8 0.7 copy-start.6
  185.8 0.8 copy-start.4
  185.8 0.8 copy-start.2
  185.8 211.7 %reduce-scatter.14.cloned.1.call-start = ((), (), s32[]{:S(2)}) async-start(), calls=%async_computation.13 | async-start | bytes 1179648 | tf_op jit(solution)/shard_map/reduce_scatter | solution.py:69
  356.2 3.3 copy-start
  359.5 38.1 %copy-start.5 = (f32[128]{0:T(128)S(1)}, f32[128]{0:T(128)}, u32[]{:S(2)}) copy-start(f32[128]{0:T(128)} %param.15) | copy-start | bytes 1540
  362.0 60.8 %all-gather.14.cloned.1.call-start = ((), (), s32[]{:S(2)}) async-start(), calls=%async_computation.14 | async-start | bytes 1179648 | tf_op jit(solution)/shard_map/all_gather | solution.py:73
  422.9 3.7 copy-start.7
  426.6 2.4 copy-start.1
Sparse Core Ops, SparseCore 0:
  10.6 39.4 all-gather.5
  52.0 36.7 all-gather.7
  90.7 36.7 all-gather.9
  129.2 36.7 all-gather.11
  168.1 43.8 reduce-scatter.5
  214.2 43.1 reduce-scatter.7
  259.8 43.1 reduce-scatter.9
  305.9 43.1 reduce-scatter.11
  362.2 35.3 reduce-scatter.13
  399.4 23.4 all-gather.13
where the time goes:
time: 440 us
  waiting for transfers between devices  316 us (72%)
  matrix products  95.5 us (22%)
  between operations  14.3 us (3%)
  other arithmetic  6.87 us (2%)
  local copies, waits for them, and re-layouts  5.62 us (1%)
    reduce_scatter x4, waiting for transfers between devices, body(): lax.psum_scatter(partial_value, 'col', scatter_dimension=0, tiled=True)  162 us
    all_gather x4, waiting for transfers between devices, body(): part = lax.all_gather(part, 'row', axis=0, tiled=True)  92.9 us
    dot_general x4, matrix products, body(): lax.dot_general(part, sensitivity, (((1,), (1,)), ((), ())), precision=la...  79.9 us
    reduce_scatter x1, waiting for transfers between devices, body(): total = lax.psum_scatter(local, 'row', scatter_dimension=0, tiled=True)  35.2 us
    all_gather x1, waiting for transfers between devices, body(): all_factor = lax.all_gather(factor, 'row', axis=0, tiled=True)  23.6 us
    dot_general x6, matrix products, pick(): lax.dot_general(left, part, (dims, ((), ())), preferred_element_type=jnp....  15.6 us
  transfers between devices with their start and end apart: 10, of which 10 were waited for; matrix products, arithmetic and copies ran while one was open for 18% of the time, Pallas kernels for 0%

commit v1 on v0

--- a/solution.py
+++ b/solution.py
@@ -70,7 +70,24 @@
     limit_col = agg_limit[:, None]
     factor = limit_col / jnp.maximum(jnp.abs(total), limit_col)
     aggregate = total * factor
-    all_factor = lax.all_gather(factor, "row", axis=0, tiled=True)
+
+    def recover_stocks(work_x):
+        link_axis = "row"
+        size_here = lax.axis_size(link_axis)
+        in_order = [(ix, (ix + 1) % size_here) for ix in range(size_here)]
+
+        def see_members_all(finding):
+            if len(finding) == size_here:
+                return finding
+            field_out = lax.ppermute(finding[0], perm=in_order, axis_name=link_axis)
+            return see_members_all([field_out, *finding])
+
+        part_now = see_members_all([work_x])
+        s_next = jnp.concatenate(part_now, 0)
+        g_now = lax.axis_index(link_axis)
+        return jnp.roll(s_next, (g_now + 1) * work_x.shape[0], 0)
+
+    all_factor = recover_stocks(factor)
     own_factor = pick(selector, split3(all_factor), ((0,), (0,)))
     return (stepped * own_factor, aggregate)
 

time: 440 us -> 452 us (1.027)
  waiting for transfers between devices: 316 us -> 330 us
    ppermute x0 -> x7, waiting for transfers between devices: none -> 37 us  [see_members_all(): field_out = lax.ppermute(finding[0], perm=in_order, axis_name=link_axis)]
    all_gather x1 -> x0, waiting for transfers between devices: 23.6 us -> none  [body(): all_factor = lax.all_gather(factor, 'row', axis=0, tiled=True)]
  transfers between devices with their start and end apart: 10 -> 16, of which waited for: 10 -> 16; matrix products, arithmetic and copies ran while one was open for 18% -> 18% of each run, Pallas kernels for 0% -> 0%
where the time goes in v1:
time: 452 us
  waiting for transfers between devices  330 us (73%)
  matrix products  94.2 us (21%)
  between operations  14.1 us (3%)
  other arithmetic  7.09 us (2%)
  local copies, waits for them, and re-layouts  5.76 us (1%)
    reduce_scatter x4, waiting for transfers between devices, body(): lax.psum_scatter(partial_value, 'col', scatter_dimension=0, tiled=True)  162 us
    all_gather x4, waiting for transfers between devices, body(): part = lax.all_gather(part, 'row', axis=0, tiled=True)  92.9 us
    dot_general x4, matrix products, body(): lax.dot_general(part, sensitivity, (((1,), (1,)), ((), ())), precision=la...  79.9 us
    ppermute x7, waiting for transfers between devices, see_members_all(): field_out = lax.ppermute(finding[0], perm=in_order, axis_name=link_axis)  37 us
    reduce_scatter x1, waiting for transfers between devices, body(): total = lax.psum_scatter(local, 'row', scatter_dimension=0, tiled=True)  35.5 us
    dot_general x6, matrix products, pick(): lax.dot_general(left, part, (dims, ((), ())), preferred_element_type=jnp....  14.4 us
  transfers between devices with their start and end apart: 16, of which 16 were waited for; matrix products, arithmetic and copies ran while one was open for 18% of the time, Pallas kernels for 0%

profile of v1, /device:TPU:0, one launch (start us, length us, event | category | flops | bytes accessed | tf_op | source)
XLA Modules:
  0.0 452.0 jit_solution(11374321473594309868)
XLA Ops:
  12.6 37.5 %all-gather.5.cloned.1.call-done = f32[256,4096]{1,0:T(8,128)} async-done(((f32[32,4096]{1,0:T(8,128)}), f32[256,4096]{1,0:T(8,128)}) %all-gather.5.cloned.1.call-update) | async-done | bytes 4194320 | tf_op jit(solution)/shard_map/all_gather | solution.py:40
  50.1 20.0 %fusion.28 = f32[256,2048]{1,0:T(8,128)} fusion(f32[256,4096]{1,0:T(8,128)} %all-gather.5.cloned.1.call-done, f32[2048,4096]{1,0:T(8,128)} %param.8), kind=kOutput, calls=%fused_computation.57 | convolution fusion | flops 12884901888 | bytes 39845888 | tf_op jit(solution)/shard_map/dot_general | solution.py:41
  70.2 18.6 %all-gather.7.cloned.1.call-done = f32[256,4096]{1,0:T(8,128)} async-done(((f32[32,4096]{1,0:T(8,128)}), f32[256,4096]{1,0:T(8,128)}) %all-gather.7.cloned.1.call-update) | async-done | bytes 4194320 | tf_op jit(solution)/shard_map/all_gather | solution.py:40
  88.8 20.0 %fusion.29 = f32[256,2048]{1,0:T(8,128)} fusion(f32[256,4096]{1,0:T(8,128)} %all-gather.7.cloned.1.call-done, f32[2048,4096]{1,0:T(8,128)} %param.8), kind=kOutput, calls=%fused_computation.58 | convolution fusion | flops 12884901888 | bytes 39845888 | tf_op jit(solution)/shard_map/dot_general | solution.py:41
  109.1 18.4 %all-gather.9.cloned.1.call-done = f32[256,4096]{1,0:T(8,128)} async-done(((f32[32,4096]{1,0:T(8,128)}), f32[256,4096]{1,0:T(8,128)}) %all-gather.9.cloned.1.call-update) | async-done | bytes 4194320 | tf_op jit(solution)/shard_map/all_gather | solution.py:40
  127.5 20.0 %fusion.30 = f32[256,2048]{1,0:T(8,128)} fusion(f32[256,4096]{1,0:T(8,128)} %all-gather.9.cloned.1.call-done, f32[2048,4096]{1,0:T(8,128)} %param.8), kind=kOutput, calls=%fused_computation.59 | convolution fusion | flops 12884901888 | bytes 39845888 | tf_op jit(solution)/shard_map/dot_general | solution.py:41
  147.5 18.4 %all-gather.11.cloned.1.call-done = f32[256,4096]{1,0:T(8,128)} async-done(((f32[32,4096]{1,0:T(8,128)}), f32[256,4096]{1,0:T(8,128)}) %all-gather.11.cloned.1.call-update) | async-done | bytes 4194320 | tf_op jit(solution)/shard_map/all_gather | solution.py:40
  165.9 19.8 %fusion.31 = f32[256,2048]{1,0:T(8,128)} fusion(f32[256,4096]{1,0:T(8,128)} %all-gather.11.cloned.1.call-done, f32[2048,4096]{1,0:T(8,128)} %param.8), kind=kOutput, calls=%fused_computation.60 | convolution fusion | flops 12884901888 | bytes 39845888 | tf_op jit(solution)/shard_map/dot_general | solution.py:41
  186.6 25.3 %reduce-scatter.6.cloned.1.call-done = f32[64,2048]{1,0:T(8,128)} async-done(((f32[256,2048]{1,0:T(8,128)}), f32[64,2048]{1,0:T(8,128)}) %reduce-scatter.6.cloned.1.call-update) | async-done | bytes 524304 | tf_op jit(solution)/shard_map/reduce_scatter | solution.py:48
  212.0 45.5 %reduce-scatter.8.cloned.1.call-done = f32[64,2048]{1,0:T(8,128)} async-done(((f32[256,2048]{1,0:T(8,128)}), f32[64,2048]{1,0:T(8,128)}) %reduce-scatter.8.cloned.1.call-update) | async-done | bytes 524304 | tf_op jit(solution)/shard_map/reduce_scatter | solution.py:48
  257.5 45.5 %reduce-scatter.10.cloned.1.call-done = f32[64,2048]{1,0:T(8,128)} async-done(((f32[256,2048]{1,0:T(8,128)}), f32[64,2048]{1,0:T(8,128)}) %reduce-scatter.10.cloned.1.call-update) | async-done | bytes 524304 | tf_op jit(solution)/shard_map/reduce_scatter | solution.py:48
  303.0 46.2 %reduce-scatter.12.cloned.1.call-done = f32[64,2048]{1,0:T(8,128)} async-done(((f32[256,2048]{1,0:T(8,128)}), f32[64,2048]{1,0:T(8,128)}) %reduce-scatter.12.cloned.1.call-update) | async-done | bytes 524304 | tf_op jit(solution)/shard_map/reduce_scatter | solution.py:48
  349.1 3.1 maximum_multiply_fusion
  359.5 2.6 fusion.19
  362.0 35.5 %reduce-scatter.14.cloned.1.call-done = f32[128,256]{1,0:T(8,128)} async-done(((f32[1024,256]{1,0:T(8,128)}), f32[128,256]{1,0:T(8,128)}) %reduce-scatter.14.cloned.1.call-update) | async-done | bytes 131088 | tf_op jit(solution)/shard_map/reduce_scatter | solution.py:69
  398.7 5.3 %collective-permute-done = f32[128,256]{1,0:T(8,128)S(1)} collective-permute-done((f32[128,256]{1,0:T(8,128)S(1)}, f32[128,256]{1,0:T(8,128)S(1)}, u32[]{:S(2)}, u32[]{:S(2)}) %collective-permute-start) | collective-permute-done | bytes 131104 | tf_op jit(solution)/shard_map/ppermute | solution.py:82
  404.0 5.3 %collective-permute-done.1 = f32[128,256]{1,0:T(8,128)S(1)} collective-permute-done((f32[128,256]{1,0:T(8,128)S(1)}, f32[128,256]{1,0:T(8,128)S(1)}, u32[]{:S(2)}, u32[]{:S(2)}) %collective-permute-start.1) | collective-permute-done | bytes 131104 | tf_op jit(solution)/shard_map/ppermute | solution.py:82
  409.3 5.3 %collective-permute-done.2 = f32[128,256]{1,0:T(8,128)S(1)} collective-permute-done((f32[128,256]{1,0:T(8,128)S(1)}, f32[128,256]{1,0:T(8,128)S(1)}, u32[]{:S(2)}, u32[]{:S(2)}) %collective-permute-start.2) | collective-permute-done | bytes 131104 | tf_op jit(solution)/shard_map/ppermute | solution.py:82
  414.6 5.3 %collective-permute-done.3 = f32[128,256]{1,0:T(8,128)S(1)} collective-permute-done((f32[128,256]{1,0:T(8,128)S(1)}, f32[128,256]{1,0:T(8,128)S(1)}, u32[]{:S(2)}, u32[]{:S(2)}) %collective-permute-start.3) | collective-permute-done | bytes 131104 | tf_op jit(solution)/shard_map/ppermute | solution.py:82
  419.9 5.3 %collective-permute-done.4 = f32[128,256]{1,0:T(8,128)S(1)} collective-permute-done((f32[128,256]{1,0:T(8,128)S(1)}, f32[128,256]{1,0:T(8,128)S(1)}, u32[]{:S(2)}, u32[]{:S(2)}) %collective-permute-start.4) | collective-permute-done | bytes 131104 | tf_op jit(solution)/shard_map/ppermute | solution.py:82
  425.1 5.3 %collective-permute-done.5 = f32[128,256]{1,0:T(8,128)S(1)} collective-permute-done((f32[128,256]{1,0:T(8,128)S(1)}, f32[128,256]{1,0:T(8,128)S(1)}, u32[]{:S(2)}, u32[]{:S(2)}) %collective-permute-start.5) | collective-permute-done | bytes 131104 | tf_op jit(solution)/shard_map/ppermute | solution.py:82
  430.4 5.3 %collective-permute-done.6 = f32[128,256]{1,0:T(8,128)S(1)} collective-permute-done((f32[128,256]{1,0:T(8,128)S(1)}, f32[128,256]{1,0:T(8,128)S(1)}, u32[]{:S(2)}, u32[]{:S(2)}) %collective-permute-start.6) | collective-permute-done | bytes 131104 | tf_op jit(solution)/shard_map/ppermute | solution.py:82
  439.3 2.4 fusion.12
  441.7 3.7 fusion.14
  (69 shorter events, 18.2 us)
Async XLA Ops:
  7.2 42.9 %all-gather.5.cloned.1.call-start = ((), (), s32[]{:S(2)}) async-start(), calls=%async_computation.5 | async-start | bytes 4718592 | tf_op jit(solution)/shard_map/all_gather | solution.py:40
  10.5 78.3 %all-gather.7.cloned.1.call-start = ((), (), s32[]{:S(2)}) async-start(), calls=%async_computation.7 | async-start | bytes 4718592 | tf_op jit(solution)/shard_map/all_gather | solution.py:40
  11.3 116.2 %all-gather.9.cloned.1.call-start = ((), (), s32[]{:S(2)}) async-start(), calls=%async_computation.9 | async-start | bytes 4718592 | tf_op jit(solution)/shard_map/all_gather | solution.py:40
  12.0 154.0 %all-gather.11.cloned.1.call-start = ((), (), s32[]{:S(2)}) async-start(), calls=%async_computation.11 | async-start | bytes 4718592 | tf_op jit(solution)/shard_map/all_gather | solution.py:40
  12.6 199.4 %reduce-scatter.6.cloned.1.call-start = ((), (), s32[]{:S(2)}) async-start(), calls=%async_computation.6 | async-start | bytes 2621440 | tf_op jit(solution)/shard_map/reduce_scatter | solution.py:48
  70.1 187.3 %reduce-scatter.8.cloned.1.call-start = ((), (), s32[]{:S(2)}) async-start(), calls=%async_computation.8 | async-start | bytes 2621440 | tf_op jit(solution)/shard_map/reduce_scatter | solution.py:48
  108.8 194.1 %reduce-scatter.10.cloned.1.call-start = ((), (), s32[]{:S(2)}) async-start(), calls=%async_computation.10 | async-start | bytes 2621440 | tf_op jit(solution)/shard_map/reduce_scatter | solution.py:48
  147.5 201.7 %reduce-scatter.12.cloned.1.call-start = ((), (), s32[]{:S(2)}) async-start(), calls=%async_computation.12 | async-start | bytes 2621440 | tf_op jit(solution)/shard_map/reduce_scatter | solution.py:48
  185.8 0.7 copy-start.4
  185.8 0.7 copy-start.7
  185.8 0.8 copy-start.5
  185.8 0.8 copy-start.3
  185.8 211.7 %reduce-scatter.14.cloned.1.call-start = ((), (), s32[]{:S(2)}) async-start(), calls=%async_computation.13 | async-start | bytes 1179648 | tf_op jit(solution)/shard_map/reduce_scatter | solution.py:69
  356.1 3.3 copy-start
  359.5 38.1 %copy-start.6 = (f32[128]{0:T(128)S(1)}, f32[128]{0:T(128)}, u32[]{:S(2)}) copy-start(f32[128]{0:T(128)} %param.15) | copy-start | bytes 1540
  397.6 38.3 %copy-start.2 = (f32[128,256]{1,0:T(8,128)S(1)}, f32[128,256]{1,0:T(8,128)}, u32[]{:S(2)}) copy-start(f32[128,256]{1,0:T(8,128)} %reduce-scatter.14.cloned.1.call-done) | copy-start | bytes 393220
  398.6 5.3 %collective-permute-start = (f32[128,256]{1,0:T(8,128)S(1)}, f32[128,256]{1,0:T(8,128)S(1)}, u32[]{:S(2)}, u32[]{:S(2)}) collective-permute-start(f32[128,256]{1,0:T(8,128)S(1)} %maximum_divide_fusion), channel_id=1, source_target_pairs={{0,4},{4,8},{8,12},{12,16},{16,20},{20,24},{24,28},{28,0},{1,5},{5... | collective-permute-start | bytes 393224 | tf_op jit(solution)/shard_map/ppermute | solution.py:82
  404.0 5.3 %collective-permute-start.1 = (f32[128,256]{1,0:T(8,128)S(1)}, f32[128,256]{1,0:T(8,128)S(1)}, u32[]{:S(2)}, u32[]{:S(2)}) collective-permute-start(f32[128,256]{1,0:T(8,128)S(1)} %collective-permute-done), channel_id=1, source_target_pairs={{0,4},{4,8},{8,12},{12,16},{16,20},{20,24},{24,28},{28,0},{1,5},{5... | collective-permute-start | bytes 393224 | tf_op jit(solution)/shard_map/ppermute | solution.py:82
  409.3 5.3 %collective-permute-start.2 = (f32[128,256]{1,0:T(8,128)S(1)}, f32[128,256]{1,0:T(8,128)S(1)}, u32[]{:S(2)}, u32[]{:S(2)}) collective-permute-start(f32[128,256]{1,0:T(8,128)S(1)} %collective-permute-done.1), channel_id=1, source_target_pairs={{0,4},{4,8},{8,12},{12,16},{16,20},{20,24},{24,28},{28,0},{1,5},{5... | collective-permute-start | bytes 393224 | tf_op jit(solution)/shard_map/ppermute | solution.py:82
  414.6 5.3 %collective-permute-start.3 = (f32[128,256]{1,0:T(8,128)S(1)}, f32[128,256]{1,0:T(8,128)S(1)}, u32[]{:S(2)}, u32[]{:S(2)}) collective-permute-start(f32[128,256]{1,0:T(8,128)S(1)} %collective-permute-done.2), channel_id=1, source_target_pairs={{0,4},{4,8},{8,12},{12,16},{16,20},{20,24},{24,28},{28,0},{1,5},{5... | collective-permute-start | bytes 393224 | tf_op jit(solution)/shard_map/ppermute | solution.py:82
  419.9 5.3 %collective-permute-start.4 = (f32[128,256]{1,0:T(8,128)S(1)}, f32[128,256]{1,0:T(8,128)S(1)}, u32[]{:S(2)}, u32[]{:S(2)}) collective-permute-start(f32[128,256]{1,0:T(8,128)S(1)} %collective-permute-done.3), channel_id=1, source_target_pairs={{0,4},{4,8},{8,12},{12,16},{16,20},{20,24},{24,28},{28,0},{1,5},{5... | collective-permute-start | bytes 393224 | tf_op jit(solution)/shard_map/ppermute | solution.py:82
  425.1 5.3 %collective-permute-start.5 = (f32[128,256]{1,0:T(8,128)S(1)}, f32[128,256]{1,0:T(8,128)S(1)}, u32[]{:S(2)}, u32[]{:S(2)}) collective-permute-start(f32[128,256]{1,0:T(8,128)S(1)} %collective-permute-done.4), channel_id=1, source_target_pairs={{0,4},{4,8},{8,12},{12,16},{16,20},{20,24},{24,28},{28,0},{1,5},{5... | collective-permute-start | bytes 393224 | tf_op jit(solution)/shard_map/ppermute | solution.py:82
  430.4 5.3 %collective-permute-start.6 = (f32[128,256]{1,0:T(8,128)S(1)}, f32[128,256]{1,0:T(8,128)S(1)}, u32[]{:S(2)}, u32[]{:S(2)}) collective-permute-start(f32[128,256]{1,0:T(8,128)S(1)} %collective-permute-done.5), channel_id=1, source_target_pairs={{0,4},{4,8},{8,12},{12,16},{16,20},{20,24},{24,28},{28,0},{1,5},{5... | collective-permute-start | bytes 393224 | tf_op jit(solution)/shard_map/ppermute | solution.py:82
  439.3 2.4 copy-start.1
Sparse Core Ops, SparseCore 0:
  10.6 39.4 all-gather.4
  52.0 36.7 all-gather.6
  90.7 36.7 all-gather.8
  129.2 36.7 all-gather.10
  168.1 43.8 reduce-scatter.5
  214.2 43.1 reduce-scatter.7
  259.7 43.1 reduce-scatter.9
  305.9 43.1 reduce-scatter.11
  362.2 35.3 reduce-scatter.13
